TPU v7x, 32 devices: a whole 2x2x4 slice. The times are simulated.
32 devices in a mesh: inp: 4 (over z), chan: 8 (over y, x, core).
Axes of the slice: x: 2, y: 2, z: 4, core: 2. Of those that a mesh axis runs over, the one named last changes fastest.
Arguments:
- samples: bfloat16 [1024, 128, 512], P('inp', 'chan'), may hold values from -16 to 16
- gram_owner: int32 [128], replicated, may hold values from 0 to 31, as said below
- beam_owner: int32 [256], replicated, may hold values from 0 to 7, as said below
- delays: float32 [256, 1024], replicated, may hold values from -64 to 64
- sections: int32 [256], replicated, may hold values from 0 to 255, each once
Outputs:
- visibilities: float32 [256, 2, 1024, 1024], P(('inp', 'chan'))
- beam_voltages: float32 [512, 4, 128, 128], P('chan', 'inp')
Inputs may be any that keep to these rules, and one draw needn't show every extreme that they name: `gram_owner`: no device owns more than 8 of the correlated channels, and some device owns exactly 8. `beam_owner`: no index of chan owns more than 64 channels, and some owns exactly 64. `sections`: each value once.
All inputs are finite; a program needn't handle non-finite values.
Results may differ from a plain program's by a relative error of at most 0.0048.
Values may be sent and summed in bfloat16 or wider, within the bound.
A program may use at most 256 MiB of HBM per device.

v0:
```python
import math

import jax
import jax.numpy as jnp
from jax import lax
from jax.sharding import PartitionSpec as P


def fourier_table(length_total):
    half_count = length_total // 2
    rows = jnp.arange(half_count, dtype=jnp.int32)
    cols = jnp.arange(length_total, dtype=jnp.int32)
    turns = (rows[:, None] * cols[None, :] % length_total).astype(jnp.float32) * (
        2.0 * math.pi / length_total
    )
    factor = 1.0 / math.sqrt(length_total)
    return jnp.stack([jnp.cos(turns) * factor, -jnp.sin(turns) * factor]).astype(jnp.bfloat16)


def slot_table(owner_list, owner_count, slot_count):
    count = owner_list.shape[0]
    places = jnp.arange(count, dtype=jnp.int32)
    before = (owner_list[None, :] == owner_list[:, None]) & (places[None, :] < places[:, None])
    slot_of = jnp.sum(before.astype(jnp.int32), axis=1)
    keys = owner_list * slot_count + slot_of
    targets = jnp.arange(owner_count * slot_count, dtype=jnp.int32)
    match = keys[None, :] == targets[:, None]
    channel_of = jnp.sum(jnp.where(match, places[None, :], 0), axis=1)
    live_slot = jnp.any(match, axis=1)
    return (keys, channel_of, live_slot)


def apply_weights(channel_data, frequencies, delay_block, length_total, inverse):
    angle = frequencies[:, None, None] * delay_block.T[None] * (2.0 * math.pi / length_total)
    real_weight = (jnp.cos(angle) * inverse).astype(jnp.bfloat16)
    imag_weight = (-jnp.sin(angle) * inverse).astype(jnp.bfloat16)
    upper = jnp.concatenate([real_weight, imag_weight], axis=-1)
    lower = jnp.concatenate([-imag_weight, real_weight], axis=-1)
    matrix = jnp.stack([upper, lower], axis=1)
    return jnp.einsum("spfm,spmc->sfc", channel_data, matrix, preferred_element_type=jnp.float32)


def shards(samples, gram_owner, beam_owner, delays, sections):
    input_count, frame_count, length_total = samples.shape
    half_count = length_total // 2
    inp_count = lax.axis_size("inp")
    chan_count = lax.axis_size("chan")
    inp_here = lax.axis_index("inp")
    chan_here = lax.axis_index("chan")
    all_inputs = input_count * inp_count
    all_frames = frame_count * chan_count
    owner_count = inp_count * chan_count
    gram_slots = 2 * gram_owner.shape[0] // owner_count
    beam_slots = 2 * half_count // chan_count
    beam_total = delays.shape[0]
    section_width = beam_total // inp_count
    table = fourier_table(length_total)
    spectra = jnp.einsum(
        "pkw,ifw->kpfi", table, samples, preferred_element_type=jnp.float32
    ).astype(jnp.bfloat16)
    _, gram_channel, gram_live = slot_table(gram_owner, owner_count, gram_slots)
    outgoing = jnp.where(
        gram_live[:, None, None, None],
        jnp.take(spectra, gram_channel, axis=0),
        jnp.zeros((), jnp.bfloat16),
    )
    outgoing = outgoing.reshape(owner_count, gram_slots, 2, frame_count, input_count)
    arrived = lax.all_to_all(outgoing, ("inp", "chan"), split_axis=0, concat_axis=0, tiled=True)
    arrived = arrived.reshape(inp_count, chan_count, gram_slots, 2, frame_count, input_count)

    def correlate(slot_index, grams):
        block = lax.dynamic_index_in_dim(arrived, slot_index, 2, keepdims=False)
        products = jnp.einsum(
            "icpfa,jcqfb->pqiajb", block, block, preferred_element_type=jnp.float32
        )
        products = products.reshape(2, 2, all_inputs, all_inputs)
        real_part = products[0, 0] + products[1, 1]
        imag_part = products[1, 0] - products[0, 1]
        result = jnp.stack([real_part, imag_part]) / all_frames
        return lax.dynamic_update_index_in_dim(grams, result, slot_index, 0)

    empty_grams = jnp.zeros((gram_slots, 2, all_inputs, all_inputs), jnp.float32)
    visibilities = lax.fori_loop(0, gram_slots, correlate, empty_grams)
    _, beam_channel, beam_live = slot_table(beam_owner, chan_count, beam_slots)
    inverse = 1.0 / math.sqrt(all_inputs)
    delay_cols = lax.dynamic_slice_in_dim(delays, inp_here * input_count, input_count, 1)
    ordered = jnp.take(delay_cols, sections, axis=0)
    leaving = jnp.where(
        beam_live[:, None, None, None],
        jnp.take(spectra, beam_channel, axis=0),
        jnp.zeros((), jnp.bfloat16),
    )
    leaving = leaving.reshape(chan_count, beam_slots, 2, frame_count, input_count)
    beam_data = lax.all_to_all(leaving, "chan", split_axis=0, concat_axis=3, tiled=True).reshape(
        beam_slots, 2, all_frames, input_count
    )
    frequencies = lax.dynamic_slice_in_dim(beam_channel, chan_here * beam_slots, beam_slots).astype(
        jnp.float32
    )
    partial_beams = apply_weights(beam_data, frequencies, ordered, length_total, inverse)
    partial_beams = partial_beams.reshape(beam_slots, all_frames, 2, beam_total)
    formed = lax.psum_scatter(partial_beams, "inp", scatter_dimension=3, tiled=True)
    formed = formed.reshape(beam_slots, all_frames, 2 * section_width)
    return (visibilities, formed.reshape(beam_slots, 1, all_frames, 2 * section_width))


def solution(mesh):
    return jax.shard_map(
        shards,
        mesh=mesh,
        in_specs=(P("inp", "chan", None), P(), P(), P(), P()),
        out_specs=(P(("inp", "chan"), None, None, None), P("chan", "inp", None, None)),
        check_vma=False,
    )
```

profile of v0, /device:TPU:9, one launch (start us, length us, event | category | flops | bytes accessed | tf_op | source)
XLA Modules:
  0.0 994.8 jit_solution(10982640282708662688)
XLA Ops:
  21.4 21.9 %gather_fusion.1 = bf16[512,2,16,256]{3,2,1,0:T(8,128)(2,1)} fusion(bf16[256,2,16,256]{3,2,1,0:T(8,128)(2,1)} %copy.45, s32[1024]{0:T(1024)S(1)} %pad_clamp_fusion.1), kind=kCustom, calls=%fused_computation.1 | custom fusion | bytes 16779264 | tf_op jit(solution)/shard_map/jit(_take)/gather | solution.py:90
  57.8 58.9 %fusion.13 = bf16[64,256,256]{2,1,0:T(8,128)(2,1)} fusion(f32[256,256]{1,0:T(8,128)S(1)} %copy.49, f32[64]{0:T(128)S(1)} %dynamic-slice_convert_fusion), kind=kLoop, calls=%fused_computation.27 | loop fusion | flops 33554432 | bytes 8651008 | tf_op jit(solution)/shard_map/neg | solution.py:38
  116.8 64.6 %multiply_convert_fusion = (bf16[64,256,256]{2,1,0:T(8,128)(2,1)}, bf16[64,256,256]{2,1,0:T(8,128)(2,1)}) fusion(f32[256,256]{1,0:T(8,128)S(1)} %copy.49, f32[64]{0:T(128)S(1)} %dynamic-slice_convert_fusion), kind=kLoop, calls=%fused_computation.18 | loop fusion | flops 29360128 | bytes 17039616 | tf_op jit(solution)/shard_map/convert_element_type | solution.py:36
  181.3 24.7 %maximum_bitcast_fusion = (bf16[64,1,256,512]{3,2,1,0:T(8,128)(2,1)}, bf16[64,1,256,512]{3,2,1,0:T(8,128)(2,1)}) fusion(bf16[64,256,256]{2,1,0:T(8,128)(2,1)} %get-tuple-element.97, bf16[64,256,256]{2,1,0:T(8,128)(2,1)} %get-tuple-element.98, bf16[64,256,256]{2,1,0:T(8,128)(2,1)} %fusion.13), kind=kLoop, calls=%fused_computation.16 | loop fusion | flops 67108864 | bytes 58720256 | tf_op jit(solution)/shard_map/stack | solution.py:39
  213.9 22.2 %fusion.4 = f32[64,128,512,1]{1,2,3,0:T(8,128)} fusion(bf16[64,2,128,256]{3,2,1,0:T(8,128)(2,1)} %bitcast.63, bf16[64,1,256,512]{3,2,1,0:T(8,128)(2,1)} %get-tuple-element.96, bf16[64,1,256,512]{3,2,1,0:T(8,128)(2,1)} %get-tuple-element.95), kind=kOutput, calls=%fused_computation.12 | convolution fusion | flops 4311744512 | bytes 58720256 | tf_op jit(solution)/shard_map/spfm,spmc->sfc/dot_general | solution.py:40
  253.4 195.2 %all-to-all-done = bf16[32,8,2,16,256]{4,3,2,1,0:T(8,128)(2,1)} async-done(((bf16[32,8,2,16,256]{4,3,2,1,0:T(8,128)(2,1)}), bf16[32,8,2,16,256]{4,3,2,1,0:T(8,128)(2,1)}, u32[]{:S(2)}, u32[]{:S(2)}) %all-to-all-start) | async-done | bytes 4194336 | tf_op jit(solution)/shard_map/all_to_all | solution.py:68
  448.6 533.7 %while.13 = (s32[]{:T(128)}, f32[8,2,1024,1024]{3,2,1,0:T(8,128)}, bf16[4,8,8,2,16,256]{5,4,3,2,1,0:T(8,128)(2,1)}, s32[]{:T(128)}) while((s32[]{:T(128)}, f32[8,2,1024,1024]{3,2,1,0:T(8,128)}, bf16[4,8,8,2,16,256]{5,4,3,2,1,0:T(8,128)(2,1)}, s32[]{:T(128)}) %tuple.46), condition=%wide.region_4.5_spmd, body=%wide.region_3.4_spmd.sunk | while | flops 1080033280 | bytes 126879288 | solution.py:83
  458.0 19.4 %copy.77 = f32[2,2,4,256,4,256]{5,4,3,2,1,0:T(4,128)} copy(f32[2,2,4,256,4,256]{3,5,0,2,1,4:T(8,128)} %convolution_bitcast_fusion.2) | data formatting | bytes 33554432 | tf_op jit(solution)/shard_map/while/body/eval_jaxpr/icpfa,jcqfb->pqiajb/transpose | solution.py:73
  477.3 20.8 %reshape.244 = f32[2,2,1024,1024]{3,2,1,0:T(8,128)} reshape(f32[2,2,4,256,4,256]{5,4,3,2,1,0:T(4,128)} %copy.77) | data formatting | bytes 33554432 | tf_op jit(solution)/shard_map/while/body/eval_jaxpr/reshape | solution.py:76
  524.9 19.4 %copy.77 = f32[2,2,4,256,4,256]{5,4,3,2,1,0:T(4,128)} copy(f32[2,2,4,256,4,256]{3,5,0,2,1,4:T(8,128)} %convolution_bitcast_fusion.2) | data formatting | bytes 33554432 | tf_op jit(solution)/shard_map/while/body/eval_jaxpr/icpfa,jcqfb->pqiajb/transpose | solution.py:73
  544.3 20.8 %reshape.244 = f32[2,2,1024,1024]{3,2,1,0:T(8,128)} reshape(f32[2,2,4,256,4,256]{5,4,3,2,1,0:T(4,128)} %copy.77) | data formatting | bytes 33554432 | tf_op jit(solution)/shard_map/while/body/eval_jaxpr/reshape | solution.py:76
  565.1 10.4 %slice_add_fusion.2 = (f32[1,1,1024,1024]{3,2,1,0:T(8,128)S(1)}, f32[1,1,1024,1024]{3,2,1,0:T(8,128)}) fusion(f32[2,2,1024,1024]{3,2,1,0:T(8,128)} %reshape.244), kind=kLoop, calls=%fused_computation.7.clone.1 | loop fusion | flops 2097152 | bytes 25165824 | tf_op jit(solution)/shard_map/while/body/eval_jaxpr/add | solution.py:77
  591.8 19.3 %copy.77 = f32[2,2,4,256,4,256]{5,4,3,2,1,0:T(4,128)} copy(f32[2,2,4,256,4,256]{3,5,0,2,1,4:T(8,128)} %convolution_bitcast_fusion.2) | data formatting | bytes 33554432 | tf_op jit(solution)/shard_map/while/body/eval_jaxpr/icpfa,jcqfb->pqiajb/transpose | solution.py:73
  611.1 20.6 %reshape.244 = f32[2,2,1024,1024]{3,2,1,0:T(8,128)} reshape(f32[2,2,4,256,4,256]{5,4,3,2,1,0:T(4,128)} %copy.77) | data formatting | bytes 33554432 | tf_op jit(solution)/shard_map/while/body/eval_jaxpr/reshape | solution.py:76
  658.5 19.3 %copy.77 = f32[2,2,4,256,4,256]{5,4,3,2,1,0:T(4,128)} copy(f32[2,2,4,256,4,256]{3,5,0,2,1,4:T(8,128)} %convolution_bitcast_fusion.2) | data formatting | bytes 33554432 | tf_op jit(solution)/shard_map/while/body/eval_jaxpr/icpfa,jcqfb->pqiajb/transpose | solution.py:73
  677.8 20.6 %reshape.244 = f32[2,2,1024,1024]{3,2,1,0:T(8,128)} reshape(f32[2,2,4,256,4,256]{5,4,3,2,1,0:T(4,128)} %copy.77) | data formatting | bytes 33554432 | tf_op jit(solution)/shard_map/while/body/eval_jaxpr/reshape | solution.py:76
  725.1 19.3 %copy.77 = f32[2,2,4,256,4,256]{5,4,3,2,1,0:T(4,128)} copy(f32[2,2,4,256,4,256]{3,5,0,2,1,4:T(8,128)} %convolution_bitcast_fusion.2) | data formatting | bytes 33554432 | tf_op jit(solution)/shard_map/while/body/eval_jaxpr/icpfa,jcqfb->pqiajb/transpose | solution.py:73
  744.4 20.6 %reshape.244 = f32[2,2,1024,1024]{3,2,1,0:T(8,128)} reshape(f32[2,2,4,256,4,256]{5,4,3,2,1,0:T(4,128)} %copy.77) | data formatting | bytes 33554432 | tf_op jit(solution)/shard_map/while/body/eval_jaxpr/reshape | solution.py:76
  791.7 19.3 %copy.77 = f32[2,2,4,256,4,256]{5,4,3,2,1,0:T(4,128)} copy(f32[2,2,4,256,4,256]{3,5,0,2,1,4:T(8,128)} %convolution_bitcast_fusion.2) | data formatting | bytes 33554432 | tf_op jit(solution)/shard_map/while/body/eval_jaxpr/icpfa,jcqfb->pqiajb/transpose | solution.py:73
  811.0 20.6 %reshape.244 = f32[2,2,1024,1024]{3,2,1,0:T(8,128)} reshape(f32[2,2,4,256,4,256]{5,4,3,2,1,0:T(4,128)} %copy.77) | data formatting | bytes 33554432 | tf_op jit(solution)/shard_map/while/body/eval_jaxpr/reshape | solution.py:76
  858.4 19.3 %copy.77 = f32[2,2,4,256,4,256]{5,4,3,2,1,0:T(4,128)} copy(f32[2,2,4,256,4,256]{3,5,0,2,1,4:T(8,128)} %convolution_bitcast_fusion.2) | data formatting | bytes 33554432 | tf_op jit(solution)/shard_map/while/body/eval_jaxpr/icpfa,jcqfb->pqiajb/transpose | solution.py:73
  877.7 20.6 %reshape.244 = f32[2,2,1024,1024]{3,2,1,0:T(8,128)} reshape(f32[2,2,4,256,4,256]{5,4,3,2,1,0:T(4,128)} %copy.77) | data formatting | bytes 33554432 | tf_op jit(solution)/shard_map/while/body/eval_jaxpr/reshape | solution.py:76
  925.0 19.3 %copy.77 = f32[2,2,4,256,4,256]{5,4,3,2,1,0:T(4,128)} copy(f32[2,2,4,256,4,256]{3,5,0,2,1,4:T(8,128)} %convolution_bitcast_fusion.2) | data formatting | bytes 33554432 | tf_op jit(solution)/shard_map/while/body/eval_jaxpr/icpfa,jcqfb->pqiajb/transpose | solution.py:73
  944.3 20.6 %reshape.244 = f32[2,2,1024,1024]{3,2,1,0:T(8,128)} reshape(f32[2,2,4,256,4,256]{5,4,3,2,1,0:T(4,128)} %copy.77) | data formatting | bytes 33554432 | tf_op jit(solution)/shard_map/while/body/eval_jaxpr/reshape | solution.py:76
  (72 shorter events, 262.6 us)
Async XLA Ops:
  7.2 49.3 %copy-start = (f32[256,1024]{1,0:T(8,128)S(1)}, f32[256,1024]{1,0:T(8,128)}, u32[]{:S(2)}) copy-start(f32[256,1024]{1,0:T(8,128)} %param.10) | copy-start | bytes 3145732
  50.8 5.6 copy-start.2
  50.8 155.2 %all-to-all-start.1 = ((bf16[8,64,2,16,256]{4,3,2,1,0:T(8,128)(2,1)}), bf16[8,64,2,16,256]{4,3,2,1,0:T(8,128)(2,1)}, u32[]{:S(2)}, u32[]{:S(2)}) async-start(bf16[8,64,2,16,256]{4,3,2,1,0:T(8,128)(2,1)} %select_select_fusion), calls=%async_computation.1 | async-start | bytes 16777216 | tf_op jit(solution)/shard_map/all_to_all | solution.py:94
  56.4 925.9 %reduce-scatter.2.cloned.1.call-start = ((), (), s32[]{:S(2)}) async-start(), calls=%async_computation.3 | async-start | bytes 20971520 | tf_op jit(solution)/shard_map/reduce_scatter | solution.py:102
  236.1 0.7 copy-start.3
  247.0 201.6 %all-to-all-start = ((bf16[32,8,2,16,256]{4,3,2,1,0:T(8,128)(2,1)}), bf16[32,8,2,16,256]{4,3,2,1,0:T(8,128)(2,1)}, u32[]{:S(2)}, u32[]{:S(2)}) async-start(bf16[32,8,2,16,256]{4,3,2,1,0:T(8,128)(2,1)} %select_select_fusion.1), calls=%async_computation | async-start | bytes 8388608 | tf_op jit(solution)/shard_map/all_to_all | solution.py:68
  982.3 5.7 copy-start.1
Sparse Core Ops, SparseCore 0:
  236.2 369.9 reduce-scatter.1
where the time goes:
time: 1010 us; the launch traced here: 995 us
  local copies, waits for them, and re-layouts  367 us (36%)
  other arithmetic  304 us (30%)
  waiting for transfers between devices  195 us (19%)
  matrix products  102 us (10%)
  between operations  14.2 us (1%)
  starting transfers between devices  12 us (1%)
    all_to_all x1, waiting for transfers between devices, shards(): lax.all_to_all(outgoing, ('inp', 'chan'), split_axis=0, concat_axis=0, ti...  195 us
    reshape x8, local copies, waits for them, and re-layouts, correlate(): products = products.reshape(2, 2, all_inputs, all_inputs)  165 us
    transpose x8, local copies, waits for them, and re-layouts, correlate(): jnp.einsum('icpfa,jcqfb->pqiajb', block, block, preferred_element_type=jn...  155 us
    add x8, other arithmetic, correlate(): real_part = products[0, 0] + products[1, 1]  82.9 us
    dot_general x8, matrix products, correlate(): jnp.einsum('icpfa,jcqfb->pqiajb', block, block, preferred_element_type=jn...  74.5 us
    convert_element_type x1, other arithmetic, apply_weights(): imag_weight = (-jnp.sin(angle) * inverse).astype(jnp.bfloat16)  64.6 us
    neg x1, other arithmetic, apply_weights(): lower = jnp.concatenate([-imag_weight, real_weight], axis=-1)  58.9 us
    dynamic_update_slice x8, other arithmetic, correlate(): return lax.dynamic_update_index_in_dim(grams, result, slot_index, 0)  56.3 us
  transfers between devices with their start and end apart: 3, of which 1 were waited for; matrix products, arithmetic and copies ran while one was open for 70% of the time, Pallas kernels for 0%

commit v1 on v0

v1 whole, which is shorter than its diff:
```python
import functools
import math

import jax
import jax.numpy as jnp
import numpy as np
from jax import lax
from jax.experimental import pallas as pl
from jax.experimental.pallas import tpu as pltpu
from jax.sharding import PartitionSpec as P

VMEM_BYTES = 56 * 1024 * 1024


def fourier_table(length_total):
    half_count = length_total // 2
    rows = np.arange(half_count, dtype=np.int32)
    cols = np.arange(length_total, dtype=np.int32)
    turns = (rows[:, None] * cols[None, :] % length_total).astype(np.float32) * np.float32(
        2.0 * math.pi / length_total
    )
    factor = np.float32(1.0 / math.sqrt(length_total))
    table = np.stack([np.cos(turns) * factor, -np.sin(turns) * factor], axis=1)
    return jnp.asarray(table.astype(jnp.bfloat16))


def slot_table(owner_list, owner_count, slot_count):
    count = owner_list.shape[0]
    places = jnp.arange(count, dtype=jnp.int32)
    before = (owner_list[None, :] == owner_list[:, None]) & (places[None, :] < places[:, None])
    slot_of = jnp.sum(before.astype(jnp.int32), axis=1)
    keys = owner_list * slot_count + slot_of
    targets = jnp.arange(owner_count * slot_count, dtype=jnp.int32)
    match = keys[None, :] == targets[:, None]
    channel_of = jnp.sum(jnp.where(match, places[None, :], 0), axis=1)
    live_slot = jnp.any(match, axis=1)
    return channel_of, live_slot


def gram_kernel(scale, data_ref, out_ref):
    inps, chans, _, _, frames, width = data_ref.shape
    parts = []
    for part in range(2):
        blocks = [
            data_ref[z, :, 0, part].reshape(chans * frames, width) for z in range(inps)
        ]
        parts.append(jnp.concatenate(blocks, axis=1))
    real, imag = parts
    both = jnp.concatenate([real, imag], axis=0)
    turned = jnp.concatenate([imag, -real], axis=0)
    tile = out_ref.shape[2]
    for lhs, part in ((both, 0), (turned, 1)):
        for row in range(0, tile, 256):
            out_ref[0, part, row : row + 256] = (
                lax.dot_general(
                    lhs[:, row : row + 256],
                    both,
                    (((0,), (0,)), ((), ())),
                    preferred_element_type=jnp.float32,
                )
                * scale
            )


def correlate(arrived, frames_total):
    inps, chans, slots, _, frames, width = arrived.shape
    total = inps * width
    return pl.pallas_call(
        functools.partial(gram_kernel, 1.0 / frames_total),
        grid=(slots,),
        in_specs=[
            pl.BlockSpec((inps, chans, 1, 2, frames, width), lambda s: (0, 0, s, 0, 0, 0))
        ],
        out_specs=pl.BlockSpec((1, 2, total, total), lambda s: (s, 0, 0, 0)),
        out_shape=jax.ShapeDtypeStruct((slots, 2, total, total), jnp.float32),
        compiler_params=pltpu.CompilerParams(vmem_limit_bytes=VMEM_BYTES),
        cost_estimate=pl.CostEstimate(
            flops=slots * 2 * 2 * total * total * 2 * chans * frames,
            bytes_accessed=slots * 2 * total * total * 4,
            transcendentals=0,
        ),
    )(arrived)


SIN_TERMS = [
    (-1) ** n * (2 * math.pi) ** (2 * n + 1) / math.factorial(2 * n + 1) for n in range(9)
]
COS_TERMS = [(-1) ** n * (2 * math.pi) ** (2 * n) / math.factorial(2 * n) for n in range(10)]


def turn_pair(turns):
    rest = turns - jnp.round(turns)
    square = rest * rest
    sine = jnp.full_like(square, SIN_TERMS[-1])
    for term in SIN_TERMS[-2::-1]:
        sine = sine * square + term
    cosine = jnp.full_like(square, COS_TERMS[-1])
    for term in COS_TERMS[-2::-1]:
        cosine = cosine * square + term
    return cosine, sine * rest


def beam_kernel(chan_axis, length_total, inverse, data_ref, delay_ref, out_ref, state, step):
    index = pl.program_id(0)
    chans, _, _, frames, width = data_ref.shape
    sects = out_ref.shape[0]
    beams = delay_ref.shape[1]

    @pl.when(index == 0)
    def _():
        first = (lax.axis_index(chan_axis) * pl.num_programs(0)).astype(jnp.float32)

        @pl.loop(0, width, step=32)
        def _(row):
            rows = pl.ds(pl.multiple_of(row, 32), 32)
            delay = delay_ref[rows]
            scaled = delay * (1.0 / length_total)
            cosine, sine = turn_pair(scaled)
            step[0, rows] = cosine
            step[1, rows] = -sine
            cosine, sine = turn_pair((first * delay) * (1.0 / length_total))
            state[0, rows] = cosine * inverse
            state[1, rows] = -sine * inverse

    real_state = state[0]
    imag_state = state[1]
    real_weight = real_state.astype(jnp.bfloat16)
    imag_weight = imag_state.astype(jnp.bfloat16)
    real_step = step[0]
    imag_step = step[1]
    state[0] = real_state * real_step - imag_state * imag_step
    state[1] = real_state * imag_step + imag_state * real_step
    half = chans * frames
    data = jnp.concatenate(
        [data_ref[:, 0, 0].reshape(half, width), data_ref[:, 0, 1].reshape(half, width)], axis=0
    )
    by_real = jnp.dot(data, real_weight, preferred_element_type=jnp.float32)
    by_imag = jnp.dot(data, imag_weight, preferred_element_type=jnp.float32)
    real_beam = by_real[:half] - by_imag[half:]
    imag_beam = by_real[half:] + by_imag[:half]
    span = beams // sects
    for sect in range(sects):
        cols = slice(sect * span, (sect + 1) * span)
        out_ref[sect, 0] = jnp.concatenate([real_beam[:, cols], imag_beam[:, cols]], axis=1).astype(
            out_ref.dtype
        )


def form_beams(data, delays, length_total, all_inputs, sects):
    chans, held, _, frames, width = data.shape
    beams = delays.shape[1]
    span = beams // sects
    return pl.pallas_call(
        functools.partial(beam_kernel, "chan", length_total, 1.0 / math.sqrt(all_inputs)),
        grid=(held,),
        in_specs=[
            pl.BlockSpec((chans, 1, 2, frames, width), lambda c: (0, c, 0, 0, 0)),
            pl.BlockSpec((width, beams), lambda c: (0, 0)),
        ],
        out_specs=pl.BlockSpec((sects, 1, chans * frames, 2 * span), lambda c: (0, c, 0, 0)),
        out_shape=jax.ShapeDtypeStruct((sects, held, chans * frames, 2 * span), jnp.bfloat16),
        scratch_shapes=[
            pltpu.VMEM((2, width, beams), jnp.float32),
            pltpu.VMEM((2, width, beams), jnp.float32),
        ],
        compiler_params=pltpu.CompilerParams(vmem_limit_bytes=VMEM_BYTES),
        cost_estimate=pl.CostEstimate(
            flops=held * 2 * 4 * chans * frames * width * beams,
            bytes_accessed=held * chans * frames * (4 * width + 4 * beams),
            transcendentals=0,
        ),
    )(data, delays)


def shards(samples, gram_owner, beam_owner, delays, sections):
    input_count, frame_count, length_total = samples.shape
    half_count = length_total // 2
    inp_count = lax.axis_size("inp")
    chan_count = lax.axis_size("chan")
    inp_here = lax.axis_index("inp")
    chan_here = lax.axis_index("chan")
    all_inputs = input_count * inp_count
    all_frames = frame_count * chan_count
    owner_count = inp_count * chan_count
    gram_slots = 2 * gram_owner.shape[0] // owner_count
    beam_slots = 2 * half_count // chan_count
    held = half_count // chan_count
    table = fourier_table(length_total)
    spectra = jnp.einsum(
        "kpw,ifw->kpfi", table, samples, preferred_element_type=jnp.float32
    ).astype(jnp.bfloat16)

    mine = spectra.reshape(chan_count, held, 2, frame_count, input_count)
    beam_data = lax.all_to_all(mine, "chan", split_axis=0, concat_axis=0, tiled=True)

    gram_channel, gram_live = slot_table(gram_owner, owner_count, gram_slots)
    outgoing = jnp.where(
        gram_live[:, None, None, None],
        jnp.take(spectra, gram_channel, axis=0),
        jnp.zeros((), jnp.bfloat16),
    )
    outgoing = outgoing.reshape(owner_count, gram_slots, 2, frame_count, input_count)
    arrived = lax.all_to_all(outgoing, ("inp", "chan"), split_axis=0, concat_axis=0, tiled=True)
    arrived = arrived.reshape(inp_count, chan_count, gram_slots, 2, frame_count, input_count)

    delay_cols = lax.dynamic_slice_in_dim(delays, inp_here * input_count, input_count, 1)
    ordered = jnp.take(delay_cols, sections, axis=0).T
    partial_beams = form_beams(beam_data, ordered, length_total, all_inputs, inp_count)
    terms = lax.all_to_all(partial_beams, "inp", split_axis=0, concat_axis=0, tiled=True)
    formed = jnp.sum(terms.astype(jnp.float32), axis=0).astype(jnp.bfloat16)
    every = lax.all_gather(formed, "chan", axis=0, tiled=True)

    visibilities = correlate(arrived, all_frames)

    beam_channel, beam_live = slot_table(beam_owner, chan_count, beam_slots)
    here = lax.dynamic_slice_in_dim(beam_channel, chan_here * beam_slots, beam_slots)
    live = lax.dynamic_slice_in_dim(beam_live, chan_here * beam_slots, beam_slots)
    voltages = jnp.where(
        live[:, None, None], jnp.take(every, here, axis=0), jnp.zeros((), jnp.bfloat16)
    ).astype(jnp.float32)
    return (visibilities, voltages[:, None])


def solution(mesh):
    return jax.shard_map(
        shards,
        mesh=mesh,
        in_specs=(P("inp", "chan", None), P(), P(), P(), P()),
        out_specs=(P(("inp", "chan"), None, None, None), P("chan", "inp", None, None)),
        check_vma=False,
    )
```

time: 1010 us -> 344 us (0.34)
  local copies, waits for them, and re-layouts: 367 us -> 15.2 us
  other arithmetic: 304 us -> 12.5 us
  matrix products: 102 us -> 5.51 us
  blocking collectives: 0 us -> 95.5 us
  waiting for transfers between devices: 195 us -> 134 us
  Pallas kernels: 0 us -> 47.3 us
    reshape x8 -> x0, local copies, waits for them, and re-layouts: 165 us -> none  [correlate(): products = products.reshape(2, 2, all_inputs, all_inputs)]
    transpose x8 -> x0, local copies, waits for them, and re-layouts: 155 us -> none  [correlate(): jnp.einsum('icpfa,jcqfb->pqiajb', block, block, preferred_element_type=jn...]
    all_to_all x1, waiting for transfers between devices: 195 us -> 90.6 us  [shards(): lax.all_to_all(outgoing, ('inp', 'chan'), split_axis=0, concat_axis=0, ti...]
    dot_general x10 -> x1, matrix products: 102 us -> 5.51 us  [shards(): jnp.einsum('kpw,ifw->kpfi', table, samples, preferred_element_type=jnp.fl...]
    all_to_all x0 -> x1, blocking collectives: none -> 95.5 us  [shards(): lax.all_to_all(partial_beams, 'inp', split_axis=0, concat_axis=0, tiled=T...]
    add x8 -> x0, other arithmetic: 82.9 us -> none  [correlate(): real_part = products[0, 0] + products[1, 1]]
    convert_element_type x2 -> x0, other arithmetic: 64.6 us -> none  [the longest x1 64.6 us: apply_weights(): imag_weight = (-jnp.sin(angle) * inverse).astype(jnp.bfloat16)]
    neg x1 -> x0, other arithmetic: 58.9 us -> none  [apply_weights(): lower = jnp.concatenate([-imag_weight, real_weight], axis=-1)]
  transfers between devices with their start and end apart: 3 -> 3, of which waited for: 1 -> 2; matrix products, arithmetic and copies ran while one was open for 70% -> 4% of each run, Pallas kernels for 0% -> 7%
where the time goes in v1:
time: 344 us; the launch traced here: 339 us
  waiting for transfers between devices  134 us (39%)
  blocking collectives  95.5 us (28%)
  Pallas kernels  47.3 us (14%)
  local copies, waits for them, and re-layouts  15.2 us (4%)
  starting transfers between devices  14.2 us (4%)
  between operations  14.2 us (4%)
  other arithmetic  12.5 us (4%)
  matrix products  5.51 us (2%)
    all_to_all x1, blocking collectives, shards(): lax.all_to_all(partial_beams, 'inp', split_axis=0, concat_axis=0, tiled=T...  95.5 us
    all_to_all x1, waiting for transfers between devices, shards(): lax.all_to_all(outgoing, ('inp', 'chan'), split_axis=0, concat_axis=0, ti...  90.6 us
    all_to_all x1, waiting for transfers between devices, shards(): lax.all_to_all(mine, 'chan', split_axis=0, concat_axis=0, tiled=True)  43.7 us
    pallas_call x1, Pallas kernels, correlate(): pl.pallas_call(functools.partial(gram_kernel, 1.0 / frames_total), grid=(...  24 us
    pallas_call x1, Pallas kernels, form_beams(): pl.pallas_call(functools.partial(beam_kernel, 'chan', length_total, 1.0 /...  23.3 us
    all_to_all x1, starting transfers between devices, shards(): lax.all_to_all(outgoing, ('inp', 'chan'), split_axis=0, concat_axis=0, ti...  8.94 us
  transfers between devices with their start and end apart: 3, of which 2 were waited for; matrix products, arithmetic and copies ran while one was open for 4% of the time, Pallas kernels for 7%

profile of v1, /device:TPU:9, one launch (start us, length us, event | category | flops | bytes accessed | tf_op | source)
XLA Modules:
  0.0 338.7 jit_solution(174186803923912356)
XLA Ops:
  7.2 5.5 %convert_bitcast_fusion = bf16[256,2,16,256]{3,0,2,1:T(8,128)(2,1)S(1)} fusion(bf16[256,2,512,1]{2,0,3,1:T(8,128)(2,1)} %constant.69, bf16[256,16,512]{2,1,0:T(8,128)(2,1)} %param.6), kind=kOutput, calls=%fused_computation.6 | convolution fusion | flops 2149580800 | bytes 8912896 | tf_op jit(solution)/shard_map/kpw,ifw->kpfi/dot_general | solution.py:189
  12.7 4.4 %copy.22 = bf16[256,2,16,256]{3,2,1,0:T(8,128)(2,1)} copy(bf16[256,2,16,256]{3,0,2,1:T(8,128)(2,1)S(1)} %convert_bitcast_fusion) | data formatting | bytes 8388608 | tf_op jit(solution)/shard_map/convert_element_type | solution.py:191
  17.1 5.3 %all-to-all-start.1 = ((bf16[8,32,2,16,256]{4,3,2,1,0:T(8,128)(2,1)}), bf16[8,32,2,16,256]{4,3,2,1,0:T(8,128)(2,1)}, u32[]{:S(2)}, u32[]{:S(2)}) async-start(bf16[8,32,2,16,256]{4,3,2,1,0:T(8,128)(2,1)} %bitcast.27), calls=%async_computation.1 | async-start | bytes 8388608 | tf_op jit(solution)/shard_map/all_to_all | solution.py:194
  22.5 1.0 gather_fusion.1
  23.5 0.1 copy.24
  23.6 0.7 select_bitcast_fusion.delay_ref
  24.3 43.7 %all-to-all-done.1.data_ref = bf16[8,32,2,16,256]{4,3,2,1,0:T(8,128)(2,1)} async-done(((bf16[8,32,2,16,256]{4,3,2,1,0:T(8,128)(2,1)}), bf16[8,32,2,16,256]{4,3,2,1,0:T(8,128)(2,1)}, u32[]{:S(2)}, u32[]{:S(2)}) %all-to-all-start.1) | async-done | bytes 4194336 | tf_op jit(solution)/shard_map/all_to_all | solution.py:194
  68.0 23.3 %shard_map.78 = bf16[4,32,128,128]{3,2,1,0:T(8,128)(2,1)} custom-call(bf16[8,32,2,16,256]{4,3,2,1,0:T(8,128)(2,1)} %all-to-all-done.1.data_ref, f32[256,256]{1,0:T(8,128)} %select_bitcast_fusion.delay_ref), custom_call_target="tpu_custom_call" | custom-call | flops 2147483648 | bytes 8388608 | tf_op jit(solution)/shard_map/pallas_call | solution.py:153
  91.4 95.5 %all_to_all.15 = bf16[4,32,128,128]{3,2,1,0:T(8,128)(2,1)} all-to-all(bf16[4,32,128,128]{3,2,1,0:T(8,128)(2,1)} %shard_map.78), channel_id=1, replica_groups=mesh['inp'=4,'chan'=8] {'inp'}, dimensions={0} | all-to-all | bytes 8388608 | tf_op jit(solution)/shard_map/all_to_all | solution.py:209
  186.9 4.3 %reduce_sum.58 = bf16[32,128,128]{2,1,0:T(8,128)(2,1)} reduce(bf16[4,32,128,128]{3,2,1,0:T(8,128)(2,1)} %all_to_all.15, bf16[]{:T(256)} %constant.41.clone.1), dimensions={0}, to_apply=%region_6.7 | reduce | flops 1572864 | bytes 5242882 | tf_op jit(solution)/shard_map/reduce_sum | solution.py:210
  191.2 0.2 convert_reduce_fusion.1
  191.4 0.1 fusion.8
  191.5 0.1 broadcast_in_dim.101
  191.6 0.1 select_reduce_fusion.1
  191.9 5.0 %gather_fusion = bf16[256,2,16,256]{3,2,1,0:T(8,128)(2,1)} fusion(bf16[256,2,16,256]{3,2,1,0:T(8,128)(2,1)} %copy.22, s32[1024]{0:T(1024)S(1)} %pad_clamp_fusion.2), kind=kCustom, calls=%fused_computation | custom fusion | bytes 8389632 | tf_op jit(solution)/shard_map/jit(_take)/gather | solution.py:199
  196.9 4.0 %select_select_fusion = bf16[32,8,2,16,256]{4,3,2,1,0:T(8,128)(2,1)} fusion(bf16[32,8,2,16,256]{4,3,2,1,0:T(8,128)(2,1)} %bitcast.28, pred[32,8]{1,0:T(8,128)(4,1)S(1)} %compare_and_fusion, pred[32,8]{1,0:T(8,128)(4,1)S(1)} %broadcast_in_dim.101), kind=kLoop, calls=%fused_computation.7 | loop fusion | flops 4194304 | bytes 8389120 | tf_op jit(solution)/shard_map/jit(_where)/select_n | solution.py:197
  200.9 8.9 %all-to-all-start = ((bf16[32,8,2,16,256]{4,3,2,1,0:T(8,128)(2,1)}), bf16[32,8,2,16,256]{4,3,2,1,0:T(8,128)(2,1)}, u32[]{:S(2)}, u32[]{:S(2)}) async-start(bf16[32,8,2,16,256]{4,3,2,1,0:T(8,128)(2,1)} %select_select_fusion), calls=%async_computation | async-start | bytes 8388608 | tf_op jit(solution)/shard_map/all_to_all | solution.py:203
  209.8 0.2 convert_reduce_fusion
  210.0 0.2 fusion.6
  210.3 0.2 select_reduce_fusion
  210.5 90.6 %all-to-all-done = bf16[32,8,2,16,256]{4,3,2,1,0:T(8,128)(2,1)} async-done(((bf16[32,8,2,16,256]{4,3,2,1,0:T(8,128)(2,1)}), bf16[32,8,2,16,256]{4,3,2,1,0:T(8,128)(2,1)}, u32[]{:S(2)}, u32[]{:S(2)}) %all-to-all-start) | async-done | bytes 4194336 | tf_op jit(solution)/shard_map/all_to_all | solution.py:203
  301.1 24.0 %shard_map.77 = f32[8,2,1024,1024]{3,2,1,0:T(8,128)} custom-call(bf16[4,8,8,2,16,256]{5,4,3,2,1,0:T(8,128)(2,1)} %bitcast.7.data_ref), custom_call_target="tpu_custom_call" | custom-call | flops 8589934592 | bytes 67108864 | tf_op jit(solution)/shard_map/pallas_call | solution.py:68
  325.1 4.3 %gather_fusion.2 = bf16[64,128,128]{2,1,0:T(8,128)(2,1)S(1)} fusion(bf16[256,128,128]{2,1,0:T(8,128)(2,1)} %all-gather.2.cloned.1.call-done, s32[1024]{0:T(1024)S(1)} %pad_clamp_fusion), kind=kCustom, calls=%fused_computation.2 | custom fusion | bytes 4194560 | tf_op jit(solution)/shard_map/jit(_take)/gather | solution.py:219
  329.4 2.5 bitcast_convert_fusion
  (24 shorter events, 0.4 us)
Async XLA Ops:
  7.2 15.3 %copy-start = (f32[256,1024]{1,0:T(8,128)S(1)}, f32[256,1024]{1,0:T(8,128)}, u32[]{:S(2)}) copy-start(f32[256,1024]{1,0:T(8,128)} %param.9) | copy-start | bytes 3145732
  17.1 5.3 %copy-start.2 = (s32[256]{0:T(256)S(1)}, s32[256]{0:T(256)}, u32[]{:S(2)}) copy-start(s32[256]{0:T(256)} %param.10) | copy-start | bytes 3076
  17.1 50.9 %all-to-all-start.1 = ((bf16[8,32,2,16,256]{4,3,2,1,0:T(8,128)(2,1)}), bf16[8,32,2,16,256]{4,3,2,1,0:T(8,128)(2,1)}, u32[]{:S(2)}, u32[]{:S(2)}) async-start(bf16[8,32,2,16,256]{4,3,2,1,0:T(8,128)(2,1)} %bitcast.27), calls=%async_computation.1 | async-start | bytes 8388608 | tf_op jit(solution)/shard_map/all_to_all | solution.py:194
  22.4 302.7 %all-gather.2.cloned.1.call-start = ((), (), s32[]{:S(2)}) async-start(), calls=%async_computation.3 | async-start | bytes 9437184 | tf_op jit(solution)/shard_map/all_gather | solution.py:211
  186.9 4.4 %copy-start.3 = (s32[128]{0:T(128)S(1)}, s32[128]{0:T(128)}, u32[]{:S(2)}) copy-start(s32[128]{0:T(128)} %param.7) | copy-start | bytes 1540
  200.9 9.0 %copy-start.1 = (s32[256]{0:T(256)S(1)}, s32[256]{0:T(256)}, u32[]{:S(2)}) copy-start(s32[256]{0:T(256)} %param.8) | copy-start | bytes 3076
  200.9 100.2 %all-to-all-start = ((bf16[32,8,2,16,256]{4,3,2,1,0:T(8,128)(2,1)}), bf16[32,8,2,16,256]{4,3,2,1,0:T(8,128)(2,1)}, u32[]{:S(2)}, u32[]{:S(2)}) async-start(bf16[32,8,2,16,256]{4,3,2,1,0:T(8,128)(2,1)} %select_select_fusion), calls=%async_computation | async-start | bytes 8388608 | tf_op jit(solution)/shard_map/all_to_all | solution.py:203
Sparse Core Ops, SparseCore 0:
  191.3 100.1 all-gather.1

commit v2 on v1

v2 whole, which is shorter than its diff:
```python
import functools
import math

import jax
import jax.numpy as jnp
import numpy as np
from jax import lax
from jax.experimental import pallas as pl
from jax.experimental.pallas import tpu as pltpu
from jax.sharding import PartitionSpec as P

VMEM_BYTES = 56 * 1024 * 1024


def fourier_table(length_total):
    half_count = length_total // 2
    rows = np.arange(half_count, dtype=np.int32)
    cols = np.arange(length_total, dtype=np.int32)
    turns = (rows[:, None] * cols[None, :] % length_total).astype(np.float32) * np.float32(
        2.0 * math.pi / length_total
    )
    factor = np.float32(1.0 / math.sqrt(length_total))
    table = np.stack([np.cos(turns) * factor, -np.sin(turns) * factor], axis=1)
    return jnp.asarray(table.astype(jnp.bfloat16))


def slot_table(owner_list, owner_count, slot_count):
    count = owner_list.shape[0]
    places = jnp.arange(count, dtype=jnp.int32)
    before = (owner_list[None, :] == owner_list[:, None]) & (places[None, :] < places[:, None])
    slot_of = jnp.sum(before.astype(jnp.int32), axis=1)
    keys = owner_list * slot_count + slot_of
    targets = jnp.arange(owner_count * slot_count, dtype=jnp.int32)
    match = keys[None, :] == targets[:, None]
    channel_of = jnp.sum(jnp.where(match, places[None, :], 0), axis=1)
    live_slot = jnp.any(match, axis=1)
    return channel_of, live_slot


def gram_kernel(scale, live_ref, data_ref, out_ref):
    live = live_ref[pl.program_id(0)] > 0

    @pl.when(jnp.logical_not(live))
    def _():
        out_ref[...] = jnp.zeros_like(out_ref)

    @pl.when(live)
    def _():
        multiply_slot(scale, data_ref, out_ref)


def multiply_slot(scale, data_ref, out_ref):
    inps, chans, _, _, frames, width = data_ref.shape
    parts = []
    for part in range(2):
        blocks = [
            data_ref[z, :, 0, part].reshape(chans * frames, width) for z in range(inps)
        ]
        parts.append(jnp.concatenate(blocks, axis=1))
    real, imag = parts
    both = jnp.concatenate([real, imag], axis=0)
    turned = jnp.concatenate([imag, -real], axis=0)
    tile = out_ref.shape[2]
    for lhs, part in ((both, 0), (turned, 1)):
        for row in range(0, tile, 256):
            out_ref[0, part, row : row + 256] = (
                lax.dot_general(
                    lhs[:, row : row + 256],
                    both,
                    (((0,), (0,)), ((), ())),
                    preferred_element_type=jnp.float32,
                )
                * scale
            )


def correlate(live, arrived, frames_total):
    inps, chans, slots, _, frames, width = arrived.shape
    total = inps * width
    return pl.pallas_call(
        functools.partial(gram_kernel, 1.0 / frames_total),
        grid_spec=pltpu.PrefetchScalarGridSpec(
            num_scalar_prefetch=1,
            grid=(slots,),
            in_specs=[
                pl.BlockSpec((inps, chans, 1, 2, frames, width), lambda s, live: (0, 0, s, 0, 0, 0))
            ],
            out_specs=pl.BlockSpec((1, 2, total, total), lambda s, live: (s, 0, 0, 0)),
        ),
        out_shape=jax.ShapeDtypeStruct((slots, 2, total, total), jnp.float32),
        compiler_params=pltpu.CompilerParams(vmem_limit_bytes=VMEM_BYTES),
        cost_estimate=pl.CostEstimate(
            flops=slots * 2 * 2 * total * total * 2 * chans * frames,
            bytes_accessed=slots * 2 * total * total * 4,
            transcendentals=0,
        ),
    )(live, arrived)


SIN_TERMS = [
    (-1) ** n * (2 * math.pi) ** (2 * n + 1) / math.factorial(2 * n + 1) for n in range(9)
]
COS_TERMS = [(-1) ** n * (2 * math.pi) ** (2 * n) / math.factorial(2 * n) for n in range(10)]


def turn_pair(turns):
    rest = turns - jnp.round(turns)
    square = rest * rest
    sine = jnp.full_like(square, SIN_TERMS[-1])
    for term in SIN_TERMS[-2::-1]:
        sine = sine * square + term
    cosine = jnp.full_like(square, COS_TERMS[-1])
    for term in COS_TERMS[-2::-1]:
        cosine = cosine * square + term
    return cosine, sine * rest


MESH = pl.DeviceIdType.MESH
GROUP = 4


def exchange_kernel(
    length_total,
    inverse,
    mine,
    outgoing,
    delay_ref,
    arrived,
    formed,
    data,
    middle,
    part,
    leaving,
    up,
    down,
    state,
    step,
    data_send,
    data_recv,
    cross_send,
    cross_recv,
    deal_send,
    deal_recv,
    up_send,
    up_recv,
    down_send,
    down_recv,
    own_sem,
):
    inps = lax.axis_size("inp")
    chans = lax.axis_size("chan")
    z = lax.axis_index("inp")
    me = lax.axis_index("chan")
    _, held, _, frames, width = mine.shape
    groups = held // GROUP
    beams = delay_ref.shape[1]
    span = beams // inps
    half = chans * frames

    barrier = pltpu.get_barrier_semaphore()
    for r in range(1, inps):
        pl.semaphore_signal(
            barrier, inc=1, device_id=(lax.rem(z + r, inps), me), device_id_type=MESH
        )

    @pl.loop(1, chans)
    def _(q):
        pl.semaphore_signal(
            barrier, inc=1, device_id=(z, lax.rem(me + q, chans)), device_id_type=MESH
        )

    pl.semaphore_wait(barrier, inps + chans - 2)

    def rows_of(g):
        return pl.ds(g * GROUP, GROUP)

    def data_copy(g, q):
        peer = lax.rem(me + q, chans)
        return pltpu.make_async_remote_copy(
            src_ref=mine.at[peer, rows_of(g)],
            dst_ref=data.at[me, rows_of(g)],
            send_sem=data_send.at[g, q],
            recv_sem=data_recv.at[g, q],
            device_id=(z, peer),
            device_id_type=MESH,
        )

    def cross_copy(r):
        peer = lax.rem(z + r, inps)
        return pltpu.make_async_remote_copy(
            src_ref=outgoing.at[peer],
            dst_ref=middle.at[r],
            send_sem=cross_send.at[r],
            recv_sem=cross_recv.at[r],
            device_id=(peer, me),
            device_id_type=MESH,
        )

    def deal_block(r):
        return outgoing.at[z] if r == 0 else middle.at[r]

    def deal_copy(r, q):
        peer = lax.rem(me + q, chans)
        return pltpu.make_async_remote_copy(
            src_ref=deal_block(r).at[peer],
            dst_ref=arrived.at[lax.rem(z + inps - r, inps), me],
            send_sem=deal_send.at[r, q],
            recv_sem=deal_recv.at[r, q],
            device_id=(z, peer),
            device_id_type=MESH,
        )

    def deal_own(r):
        return pltpu.make_async_copy(
            deal_block(r).at[me],
            arrived.at[lax.rem(z + inps - r, inps), me],
            own_sem.at[r],
        )

    def up_copy(d, g):
        return pltpu.make_async_remote_copy(
            src_ref=leaving.at[d, rows_of(g)],
            dst_ref=up.at[d, rows_of(g)],
            send_sem=up_send.at[d, g],
            recv_sem=up_recv.at[d, g],
            device_id=(lax.rem(z + 1, inps), me),
            device_id_type=MESH,
        )

    def down_copy(d, g):
        return pltpu.make_async_remote_copy(
            src_ref=leaving.at[d, rows_of(g)],
            dst_ref=down.at[d, rows_of(g)],
            send_sem=down_send.at[d, g],
            recv_sem=down_recv.at[d, g],
            device_id=(lax.rem(z + inps - 1, inps), me),
            device_id_type=MESH,
        )

    own_data = pltpu.make_async_copy(mine.at[me], data.at[me], own_sem.at[inps])
    own_data.start()

    @pl.loop(1, chans)
    def _(q):
        data_copy(0, q).start()

    for r in range(1, inps):
        cross_copy(r).start()

    @pl.loop(1, groups)
    def _(g):
        @pl.loop(1, chans)
        def _(q):
            data_copy(g, q).start()

    def deal(r):
        deal_own(r).start()

        @pl.loop(1, chans)
        def _(q):
            deal_copy(r, q).start()

    deal(0)

    first = (me * held).astype(jnp.float32)

    @pl.loop(0, width // 32)
    def _(block):
        rows = pl.ds(pl.multiple_of(block * 32, 32), 32)
        delay = delay_ref[rows]
        cosine, sine = turn_pair(delay * (1.0 / length_total))
        step[0, rows] = cosine
        step[1, rows] = -sine
        cosine, sine = turn_pair((first * delay) * (1.0 / length_total))
        state[0, rows] = cosine * inverse
        state[1, rows] = -sine * inverse

    own_data.wait()

    def compute(g):
        @pl.loop(1, chans)
        def _(q):
            data_copy(g, q).wait_recv()

        @pl.loop(0, GROUP)
        def _(offset):
            c = g * GROUP + offset
            real_state = state[0]
            imag_state = state[1]
            real_weight = real_state.astype(jnp.bfloat16)
            imag_weight = imag_state.astype(jnp.bfloat16)
            real_step = step[0]
            imag_step = step[1]
            state[0] = real_state * real_step - imag_state * imag_step
            state[1] = real_state * imag_step + imag_state * real_step
            both = jnp.concatenate(
                [data[:, c, 0].reshape(half, width), data[:, c, 1].reshape(half, width)], axis=0
            )
            by_real = jnp.dot(both, real_weight, preferred_element_type=jnp.float32)
            by_imag = jnp.dot(both, imag_weight, preferred_element_type=jnp.float32)
            real_beam = by_real[:half] - by_imag[half:]
            imag_beam = by_real[half:] + by_imag[:half]
            for d in range(inps):
                cols = slice(d * span, (d + 1) * span)
                part[d, c] = jnp.concatenate([real_beam[:, cols], imag_beam[:, cols]], axis=1)

    def relay(g):
        rows = rows_of(g)
        for d in range(inps - 1, 0, -1):

            @pl.when(z < d)
            def _():
                @pl.when(z == 0)
                def _():
                    leaving[d, rows] = part[d, rows].astype(jnp.bfloat16)

                @pl.when(z > 0)
                def _():
                    up_copy(d, g).wait_recv()
                    leaving[d, rows] = (
                        part[d, rows] + up[d, rows].astype(jnp.float32)
                    ).astype(jnp.bfloat16)

                up_copy(d, g).start()

        for d in range(inps - 1):

            @pl.when(z > d)
            def _():
                @pl.when(z == inps - 1)
                def _():
                    leaving[d, rows] = part[d, rows].astype(jnp.bfloat16)

                @pl.when(z < inps - 1)
                def _():
                    down_copy(d, g).wait_recv()
                    leaving[d, rows] = (
                        part[d, rows] + down[d, rows].astype(jnp.float32)
                    ).astype(jnp.bfloat16)

                down_copy(d, g).start()

        for d in range(inps):

            @pl.when(z == d)
            def _():
                total = part[d, rows]
                if d > 0:
                    up_copy(d, g).wait_recv()
                    total = total + up[d, rows].astype(jnp.float32)
                if d < inps - 1:
                    down_copy(d, g).wait_recv()
                    total = total + down[d, rows].astype(jnp.float32)
                formed[rows] = total.astype(jnp.bfloat16)

    compute(0)

    @pl.loop(1, groups)
    def _(g):
        compute(g)
        relay(g - 1)

    def forward(r):
        cross_copy(r).wait_recv()
        deal(r)

    for r in range(1, inps):
        forward(r)
    relay(groups - 1)

    for r in range(1, inps):
        cross_copy(r).wait_send()
    for r in range(inps):
        deal_own(r).wait()

        @pl.loop(1, chans)
        def _(q):
            deal_copy(r, q).wait()

    @pl.loop(0, groups)
    def _(g):
        @pl.loop(1, chans)
        def _(q):
            data_copy(g, q).wait_send()

        for d in range(1, inps):

            @pl.when(z < d)
            def _():
                up_copy(d, g).wait_send()

        for d in range(inps - 1):

            @pl.when(z > d)
            def _():
                down_copy(d, g).wait_send()


def exchange(mine, outgoing, delays, length_total, all_inputs):
    inps = outgoing.shape[0]
    chans, held, _, frames, width = mine.shape
    beams = delays.shape[1]
    groups = held // GROUP
    formed_shape = (held, chans * frames, 2 * beams // inps)
    dma = pltpu.SemaphoreType.DMA
    return pl.pallas_call(
        functools.partial(exchange_kernel, length_total, 1.0 / math.sqrt(all_inputs)),
        in_specs=[
            pl.BlockSpec(memory_space=pl.ANY),
            pl.BlockSpec(memory_space=pl.ANY),
            pl.BlockSpec(memory_space=pltpu.VMEM),
        ],
        out_specs=[
            pl.BlockSpec(memory_space=pl.ANY),
            pl.BlockSpec(memory_space=pltpu.VMEM),
        ],
        out_shape=[
            jax.ShapeDtypeStruct(outgoing.shape, jnp.bfloat16),
            jax.ShapeDtypeStruct(formed_shape, jnp.bfloat16),
        ],
        scratch_shapes=[
            pltpu.VMEM(mine.shape, jnp.bfloat16),
            pltpu.VMEM(outgoing.shape, jnp.bfloat16),
            pltpu.VMEM((inps, *formed_shape), jnp.float32),
            pltpu.VMEM((inps, *formed_shape), jnp.bfloat16),
            pltpu.VMEM((inps, *formed_shape), jnp.bfloat16),
            pltpu.VMEM((inps, *formed_shape), jnp.bfloat16),
            pltpu.VMEM((2, width, beams), jnp.float32),
            pltpu.VMEM((2, width, beams), jnp.float32),
            dma((groups, chans)),
            dma((groups, chans)),
            dma((inps,)),
            dma((inps,)),
            dma((inps, chans)),
            dma((inps, chans)),
            dma((inps, groups)),
            dma((inps, groups)),
            dma((inps, groups)),
            dma((inps, groups)),
            dma((inps + 1,)),
        ],
        compiler_params=pltpu.CompilerParams(
            collective_id=0, has_side_effects=True, vmem_limit_bytes=VMEM_BYTES
        ),
        cost_estimate=pl.CostEstimate(
            flops=held * 2 * 4 * chans * frames * width * beams,
            bytes_accessed=held * chans * frames * (4 * width + 4 * beams),
            transcendentals=0,
        ),
    )(mine, outgoing, delays)


def shards(samples, gram_owner, beam_owner, delays, sections):
    input_count, frame_count, length_total = samples.shape
    half_count = length_total // 2
    inp_count = lax.axis_size("inp")
    chan_count = lax.axis_size("chan")
    inp_here = lax.axis_index("inp")
    chan_here = lax.axis_index("chan")
    all_inputs = input_count * inp_count
    all_frames = frame_count * chan_count
    owner_count = inp_count * chan_count
    gram_slots = 2 * gram_owner.shape[0] // owner_count
    beam_slots = 2 * half_count // chan_count
    held = half_count // chan_count
    table = fourier_table(length_total)
    spectra = jnp.einsum(
        "kpw,ifw->kpfi", table, samples, preferred_element_type=jnp.float32
    ).astype(jnp.bfloat16)

    mine = spectra.reshape(chan_count, held, 2, frame_count, input_count)
    gram_channel, gram_live = slot_table(gram_owner, owner_count, gram_slots)
    outgoing = jnp.take(spectra, gram_channel, axis=0).reshape(
        inp_count, chan_count, gram_slots, 2, frame_count, input_count
    )
    gram_live = gram_live.astype(jnp.int32).reshape(owner_count, gram_slots)
    gram_live = lax.dynamic_index_in_dim(gram_live, inp_here * chan_count + chan_here, 0, False)

    delay_cols = lax.dynamic_slice_in_dim(delays, inp_here * input_count, input_count, 1)
    ordered = jnp.take(delay_cols, sections, axis=0).T
    arrived, formed = exchange(mine, outgoing, ordered, length_total, all_inputs)
    every = lax.all_gather(formed, "chan", axis=0, tiled=True)

    visibilities = correlate(gram_live, arrived, all_frames)

    beam_channel, beam_live = slot_table(beam_owner, chan_count, beam_slots)
    here = lax.dynamic_slice_in_dim(beam_channel, chan_here * beam_slots, beam_slots)
    live = lax.dynamic_slice_in_dim(beam_live, chan_here * beam_slots, beam_slots)
    voltages = jnp.where(
        live[:, None, None], jnp.take(every, here, axis=0), jnp.zeros((), jnp.bfloat16)
    ).astype(jnp.float32)
    return (visibilities, voltages[:, None])


def solution(mesh):
    return jax.shard_map(
        shards,
        mesh=mesh,
        in_specs=(P("inp", "chan", None), P(), P(), P(), P()),
        out_specs=(P(("inp", "chan"), None, None, None), P("chan", "inp", None, None)),
        check_vma=False,
    )
```

time: 344 us -> 342 us (level); the launches traced: 339 us -> 340 us
  Pallas kernels: 47.3 us -> 265 us
  waiting for transfers between devices: 134 us -> 28.6 us
  blocking collectives: 95.5 us -> 0 us
  starting transfers between devices: 14.2 us -> 0.04 us
    pallas_call x2, Pallas kernels: 47.3 us -> 265 us  [the longest x1 240 us: exchange(): pl.pallas_call(functools.partial(exchange_kernel, length_total, 1.0 / mat...]
    all_to_all x2 -> x0, waiting for transfers between devices: 134 us -> none  [the longest x1 90.6 us: shards(): lax.all_to_all(outgoing, ('inp', 'chan'), split_axis=0, concat_axis=0, ti...]
    all_to_all x1 -> x0, blocking collectives: 95.5 us -> none  [shards(): lax.all_to_all(partial_beams, 'inp', split_axis=0, concat_axis=0, tiled=T...]
    all_gather x1, waiting for transfers between devices: 0.01 us -> 28.5 us  [shards(): every = lax.all_gather(formed, 'chan', axis=0, tiled=True)]
    all_to_all x2 -> x0, starting transfers between devices: 14.2 us -> none  [the longest x1 8.94 us: shards(): lax.all_to_all(outgoing, ('inp', 'chan'), split_axis=0, concat_axis=0, ti...]
    reduce_sum x1 -> x0, other arithmetic: 4.33 us -> none  [shards(): formed = jnp.sum(terms.astype(jnp.float32), axis=0).astype(jnp.bfloat16)]
    select_n x1 -> x0, other arithmetic: 3.97 us -> none  [shards(): jnp.where(gram_live[:, None, None, None], jnp.take(spectra, gram_channel,...]
    select_n x1 -> x2, other arithmetic: 0.01 us -> 3.88 us  [shards(): jnp.take(spectra, gram_channel, axis=0)]
  transfers between devices with their start and end apart: 3 -> 1, of which waited for: 2 -> 1; matrix products, arithmetic and copies ran while one was open for 4% -> 0% of each run, Pallas kernels for 7% -> 8%
where the time goes in v2:
time: 342 us; the launch traced here: 340 us
  Pallas kernels  265 us (77%)
  waiting for transfers between devices  28.6 us (8%)
  local copies, waits for them, and re-layouts  15.7 us (5%)
  between operations  14.2 us (4%)
  other arithmetic  10.9 us (3%)
  matrix products  5.48 us (2%)
    pallas_call x1, Pallas kernels, exchange(): pl.pallas_call(functools.partial(exchange_kernel, length_total, 1.0 / mat...  240 us
    all_gather x1, waiting for transfers between devices, shards(): every = lax.all_gather(formed, 'chan', axis=0, tiled=True)  28.5 us
    pallas_call x1, Pallas kernels, correlate(): pl.pallas_call(functools.partial(gram_kernel, 1.0 / frames_total), grid_s...  25.6 us
  transfers between devices with their start and end apart: 1, of which 1 were waited for; matrix products, arithmetic and copies ran while one was open for 0% of the time, Pallas kernels for 8%

profile of v2, /device:TPU:9, one launch (start us, length us, event | category | flops | bytes accessed | tf_op | source)
XLA Modules:
  0.0 340.3 jit_solution(17631641358108108324)
XLA Ops:
  7.2 0.8 compare_and_fusion.2
  8.0 0.7 compare_select_fusion.2
  8.7 0.9 convert_reduce_fusion.1
  9.6 0.7 multiply_add_fusion.1
  10.2 0.1 select_reduce_fusion.1
  10.4 0.1 reduce_sum.42
  10.6 1.0 gather_fusion.1
  11.5 0.1 copy.26
  11.7 5.5 %convert_bitcast_fusion = bf16[256,2,16,256]{3,0,2,1:T(8,128)(2,1)S(1)} fusion(bf16[256,2,512,1]{2,0,3,1:T(8,128)(2,1)} %constant.73, bf16[256,16,512]{2,1,0:T(8,128)(2,1)} %param.6), kind=kOutput, calls=%fused_computation.6 | convolution fusion | flops 2149580800 | bytes 8912896 | tf_op jit(solution)/shard_map/kpw,ifw->kpfi/dot_general | solution.py:467
  17.1 4.4 %copy.24 = bf16[256,2,16,256]{3,2,1,0:T(8,128)(2,1)} copy(bf16[256,2,16,256]{3,0,2,1:T(8,128)(2,1)S(1)} %convert_bitcast_fusion) | data formatting | bytes 8388608 | tf_op jit(solution)/shard_map/convert_element_type | solution.py:469
  21.6 0.7 select_bitcast_fusion.delay_ref
  22.3 5.0 %gather_fusion = bf16[256,2,16,256]{3,2,1,0:T(8,128)(2,1)} fusion(bf16[256,2,16,256]{3,2,1,0:T(8,128)(2,1)} %copy.24, s32[1024]{0:T(1024)S(1)} %pad_clamp_fusion.2), kind=kCustom, calls=%fused_computation | custom fusion | bytes 8389632 | tf_op jit(solution)/shard_map/jit(_take)/gather | solution.py:473
  27.3 3.9 %broadcast_select_fusion.outgoing = bf16[4,8,8,2,16,256]{5,4,3,2,1,0:T(8,128)(2,1)} fusion(bf16[4,8,8,2,16,256]{5,4,3,2,1,0:T(8,128)(2,1)} %bitcast.29, pred[4,8,8]{2,1,0:T(8,128)(4,1)S(1)} %compare_and_fusion), kind=kLoop, calls=%fused_computation.7 | loop fusion | flops 2097152 | bytes 8388864 | tf_op jit(solution)/shard_map/jit(_take)/select_n | solution.py:473
  31.2 239.9 %shard_map.77 = (bf16[4,8,8,2,16,256]{5,4,3,2,1,0:T(8,128)(2,1)}, bf16[32,128,128]{2,1,0:T(8,128)(2,1)}) custom-call(bf16[8,32,2,16,256]{4,3,2,1,0:T(8,128)(2,1)} %bitcast.28, bf16[4,8,8,2,16,256]{5,4,3,2,1,0:T(8,128)(2,1)} %broadcast_select_fusion.outgoing, f32[256,256]{1,0:T(8,128)} %select_bitcast_fusion.delay_ref), custom_call_target="tpu_custom_call" | custom-call | flops 2147483648 | bytes 8388608 | tf_op jit(solution)/shard_map/pallas_call | solution.py:406
  271.1 0.1 fusion.8
  271.3 0.2 convert_reduce_fusion
  271.5 0.2 fusion.6
  271.8 0.5 dynamic-slice_bitcast_fusion.live_ref
  272.3 0.1 select_reduce_fusion
  272.4 0.1 compare_and_fusion.1
  272.5 25.6 %shard_map.78 = f32[8,2,1024,1024]{3,2,1,0:T(8,128)} custom-call(s32[8]{0:T(128)} %dynamic-slice_bitcast_fusion.live_ref, bf16[4,8,8,2,16,256]{5,4,3,2,1,0:T(8,128)(2,1)} %get-tuple-element.4.data_ref), custom_call_target="tpu_custom_call" | custom-call | flops 8589934592 | bytes 67108864 | tf_op jit(solution)/shard_map/pallas_call | solution.py:80
  298.1 28.5 %all-gather.2.cloned.1.call-done = bf16[256,128,128]{2,1,0:T(8,128)(2,1)} async-done(((bf16[32,128,128]{2,1,0:T(8,128)(2,1)}), bf16[256,128,128]{2,1,0:T(8,128)(2,1)}) %all-gather.2.cloned.1.call-update) | async-done | bytes 8388624 | tf_op jit(solution)/shard_map/all_gather | solution.py:482
  326.6 4.3 %gather_fusion.2 = bf16[64,128,128]{2,1,0:T(8,128)(2,1)S(1)} fusion(bf16[256,128,128]{2,1,0:T(8,128)(2,1)} %all-gather.2.cloned.1.call-done, s32[1024]{0:T(1024)S(1)} %pad_clamp_fusion), kind=kCustom, calls=%fused_computation.2 | custom fusion | bytes 4194560 | tf_op jit(solution)/shard_map/jit(_take)/gather | solution.py:490
  331.0 2.5 bitcast_convert_fusion
  (16 shorter events, 0.3 us)
Async XLA Ops:
  7.2 3.3 copy-start
  7.2 319.5 %all-gather.2.cloned.1.call-start = ((), (), s32[]{:S(2)}) async-start(), calls=%async_computation | async-start | bytes 9437184 | tf_op jit(solution)/shard_map/all_gather | solution.py:482
  31.2 240.1 %copy-start.1 = (s32[256]{0:T(256)S(1)}, s32[256]{0:T(256)}, u32[]{:S(2)}) copy-start(s32[256]{0:T(256)} %param.8) | copy-start | bytes 3076
Sparse Core Ops, SparseCore 0:
  271.2 55.3 all-gather.1

commit v3 on v2

--- a/solution.py
+++ b/solution.py
@@ -185,13 +185,14 @@
             device_id_type=MESH,
         )
 
-    def cross_copy(r):
+    def cross_copy(r, q):
         peer = lax.rem(z + r, inps)
+        target = lax.rem(me + q, chans)
         return pltpu.make_async_remote_copy(
-            src_ref=outgoing.at[peer],
-            dst_ref=middle.at[r],
-            send_sem=cross_send.at[r],
-            recv_sem=cross_recv.at[r],
+            src_ref=outgoing.at[peer, target],
+            dst_ref=middle.at[r, target],
+            send_sem=cross_send.at[r, q],
+            recv_sem=cross_recv.at[r, q],
             device_id=(peer, me),
             device_id_type=MESH,
         )
@@ -239,28 +240,38 @@
 
     own_data = pltpu.make_async_copy(mine.at[me], data.at[me], own_sem.at[inps])
     own_data.start()
-
-    @pl.loop(1, chans)
-    def _(q):
-        data_copy(0, q).start()
-
-    for r in range(1, inps):
-        cross_copy(r).start()
-
-    @pl.loop(1, groups)
-    def _(g):
+    share = chans // groups
+
+    def send_data(g):
         @pl.loop(1, chans)
         def _(q):
             data_copy(g, q).start()
 
-    def deal(r):
-        deal_own(r).start()
-
-        @pl.loop(1, chans)
+    def send_cross(g):
+        @pl.loop(g * share, (g + 1) * share)
         def _(q):
-            deal_copy(r, q).start()
-
-    deal(0)
+            for r in range(1, inps):
+                cross_copy(r, q).start()
+
+    def deal_on(g):
+        @pl.loop(g * share, (g + 1) * share)
+        def _(q):
+            for r in range(1, inps):
+                cross_copy(r, q).wait_recv()
+
+            @pl.when(q == 0)
+            def _():
+                for r in range(inps):
+                    deal_own(r).start()
+
+            @pl.when(q > 0)
+            def _():
+                for r in range(inps):
+                    deal_copy(r, q).start()
+
+    send_data(0)
+    send_cross(0)
+    send_data(1)
 
     first = (me * held).astype(jnp.float32)
 
@@ -304,7 +315,7 @@
                 cols = slice(d * span, (d + 1) * span)
                 part[d, c] = jnp.concatenate([real_beam[:, cols], imag_beam[:, cols]], axis=1)
 
-    def relay(g):
+    def pass_up(g):
         rows = rows_of(g)
         for d in range(inps - 1, 0, -1):
 
@@ -323,6 +334,8 @@
 
                 up_copy(d, g).start()
 
+    def pass_down(g):
+        rows = rows_of(g)
         for d in range(inps - 1):
 
             @pl.when(z > d)
@@ -340,6 +353,8 @@
 
                 down_copy(d, g).start()
 
+    def finish(g):
+        rows = rows_of(g)
         for d in range(inps):
 
             @pl.when(z == d)
@@ -353,23 +368,45 @@
                     total = total + down[d, rows].astype(jnp.float32)
                 formed[rows] = total.astype(jnp.bfloat16)
 
-    compute(0)
-
-    @pl.loop(1, groups)
-    def _(g):
-        compute(g)
-        relay(g - 1)
-
-    def forward(r):
-        cross_copy(r).wait_recv()
-        deal(r)
-
-    for r in range(1, inps):
-        forward(r)
-    relay(groups - 1)
-
-    for r in range(1, inps):
-        cross_copy(r).wait_send()
+    @pl.loop(0, groups + inps)
+    def _(turn):
+        @pl.when(turn + 2 < groups)
+        def _():
+            send_data(turn + 2)
+
+        @pl.when(turn < groups)
+        def _():
+            compute(turn)
+
+        up_group = turn - z
+
+        @pl.when((up_group >= 0) & (up_group < groups))
+        def _():
+            pass_up(up_group)
+
+        down_group = turn - (inps - 1 - z)
+
+        @pl.when((down_group >= 0) & (down_group < groups))
+        def _():
+            pass_down(down_group)
+
+        @pl.when(turn + 1 < groups)
+        def _():
+            send_cross(turn + 1)
+
+        @pl.when((turn >= 2) & (turn - 2 < groups))
+        def _():
+            deal_on(turn - 2)
+
+        @pl.when(turn >= inps)
+        def _():
+            finish(turn - inps)
+
+    @pl.loop(0, chans)
+    def _(q):
+        for r in range(1, inps):
+            cross_copy(r, q).wait_send()
+
     for r in range(inps):
         deal_own(r).wait()
 
@@ -429,8 +466,8 @@
             pltpu.VMEM((2, width, beams), jnp.float32),
             dma((groups, chans)),
             dma((groups, chans)),
-            dma((inps,)),
-            dma((inps,)),
+            dma((inps, chans)),
+            dma((inps, chans)),
             dma((inps, chans)),
             dma((inps, chans)),
             dma((inps, groups)),
@@ -470,14 +507,14 @@
 
     mine = spectra.reshape(chan_count, held, 2, frame_count, input_count)
     gram_channel, gram_live = slot_table(gram_owner, owner_count, gram_slots)
-    outgoing = jnp.take(spectra, gram_channel, axis=0).reshape(
+    outgoing = jnp.take(spectra, gram_channel, axis=0, mode="clip").reshape(
         inp_count, chan_count, gram_slots, 2, frame_count, input_count
     )
     gram_live = gram_live.astype(jnp.int32).reshape(owner_count, gram_slots)
     gram_live = lax.dynamic_index_in_dim(gram_live, inp_here * chan_count + chan_here, 0, False)
 
     delay_cols = lax.dynamic_slice_in_dim(delays, inp_here * input_count, input_count, 1)
-    ordered = jnp.take(delay_cols, sections, axis=0).T
+    ordered = jnp.take(delay_cols, sections, axis=0, mode="clip").T
     arrived, formed = exchange(mine, outgoing, ordered, length_total, all_inputs)
     every = lax.all_gather(formed, "chan", axis=0, tiled=True)
 
@@ -487,7 +524,7 @@
     here = lax.dynamic_slice_in_dim(beam_channel, chan_here * beam_slots, beam_slots)
     live = lax.dynamic_slice_in_dim(beam_live, chan_here * beam_slots, beam_slots)
     voltages = jnp.where(
-        live[:, None, None], jnp.take(every, here, axis=0), jnp.zeros((), jnp.bfloat16)
+        live[:, None, None], jnp.take(every, here, axis=0, mode="clip"), jnp.zeros((), jnp.bfloat16)
     ).astype(jnp.float32)
     return (visibilities, voltages[:, None])
 

time: 342 us -> 258 us (0.75)
  Pallas kernels: 265 us -> 190 us
  other arithmetic: 10.9 us -> 5.38 us
  waiting for transfers between devices: 28.6 us -> 25.1 us
    pallas_call x1, Pallas kernels: 240 us -> 164 us  [exchange(): pl.pallas_call(functools.partial(exchange_kernel, length_total, 1.0 / mat...]
    select_n x4 -> x0, other arithmetic: 5.27 us -> none  [the longest x2 3.88 us: shards(): jnp.take(spectra, gram_channel, axis=0)]
    all_gather x1, waiting for transfers between devices: 28.5 us -> 25 us  [shards(): every = lax.all_gather(formed, 'chan', axis=0, tiled=True)]
  transfers between devices with their start and end apart: 1 -> 1, of which waited for: 1 -> 1; matrix products, arithmetic and copies ran while one was open for 0% -> 1% of each run, Pallas kernels for 8% -> 10%
where the time goes in v3:
time: 258 us; the launch traced here: 257 us
  Pallas kernels  190 us (74%)
  waiting for transfers between devices  25.1 us (10%)
  local copies, waits for them, and re-layouts  16.4 us (6%)
  between operations  14.1 us (5%)
  matrix products  5.46 us (2%)
  other arithmetic  5.38 us (2%)
    pallas_call x1, Pallas kernels, exchange(): pl.pallas_call(functools.partial(exchange_kernel, length_total, 1.0 / mat...  164 us
    pallas_call x1, Pallas kernels, correlate(): pl.pallas_call(functools.partial(gram_kernel, 1.0 / frames_total), grid_s...  26.5 us
    all_gather x1, waiting for transfers between devices, shards(): every = lax.all_gather(formed, 'chan', axis=0, tiled=True)  25 us
    dot_general x1, matrix products, shards(): jnp.einsum('kpw,ifw->kpfi', table, samples, preferred_element_type=jnp.fl...  5.46 us
  transfers between devices with their start and end apart: 1, of which 1 were waited for; matrix products, arithmetic and copies ran while one was open for 1% of the time, Pallas kernels for 10%

profile of v3, /device:TPU:9, one launch (start us, length us, event | category | flops | bytes accessed | tf_op | source)
XLA Modules:
  0.0 256.9 jit_solution(7874353721673215280)
XLA Ops:
  7.2 0.0 all-gather.2.cloned.1.call-start
  7.2 0.9 convert_reduce_fusion.1
  8.2 0.7 multiply_add_fusion.1
  8.8 0.1 select_reduce_fusion.1
  8.9 0.7 pad_clamp_fusion.1
  9.7 1.0 gather_fusion.1
  10.6 0.8 copy.26
  11.5 5.5 %convert_bitcast_fusion = bf16[256,2,16,256]{3,0,2,1:T(8,128)(2,1)S(1)} fusion(bf16[256,2,512,1]{2,0,3,1:T(8,128)(2,1)} %constant.34, bf16[256,16,512]{2,1,0:T(8,128)(2,1)} %param.6), kind=kOutput, calls=%fused_computation.6 | convolution fusion | flops 2149580800 | bytes 8912896 | tf_op jit(solution)/shard_map/kpw,ifw->kpfi/dot_general | solution.py:504
  16.9 4.4 %copy.24 = bf16[256,2,16,256]{3,2,1,0:T(8,128)(2,1)} copy(bf16[256,2,16,256]{3,0,2,1:T(8,128)(2,1)S(1)} %convert_bitcast_fusion) | data formatting | bytes 8388608 | tf_op jit(solution)/shard_map/convert_element_type | solution.py:506
  21.4 5.0 %gather_fusion = bf16[256,2,16,256]{3,2,1,0:T(8,128)(2,1)} fusion(bf16[256,2,16,256]{3,2,1,0:T(8,128)(2,1)} %copy.24, s32[1024]{0:T(1024)S(1)} %pad_clamp_fusion.2), kind=kCustom, calls=%fused_computation | custom fusion | bytes 8389632 | tf_op jit(solution)/shard_map/jit(_take)/gather | solution.py:510
  26.4 164.0 %shard_map.77 = (bf16[4,8,8,2,16,256]{5,4,3,2,1,0:T(8,128)(2,1)}, bf16[32,128,128]{2,1,0:T(8,128)(2,1)}) custom-call(bf16[8,32,2,16,256]{4,3,2,1,0:T(8,128)(2,1)} %bitcast.23, bf16[4,8,8,2,16,256]{5,4,3,2,1,0:T(8,128)(2,1)} %bitcast.24, f32[256,256]{1,0:T(8,128)} %bitcast.25), custom_call_target="tpu_custom_call" | custom-call | flops 2147483648 | bytes 8388608 | tf_op jit(solution)/shard_map/pallas_call | solution.py:443
  190.4 0.0 all-gather.2.cloned.1.call-update
  190.4 0.1 fusion.7
  190.5 0.2 convert_reduce_fusion
  190.7 0.2 fusion.5
  190.9 0.1 dynamic_slice.15
  191.0 0.2 select_reduce_fusion
  191.1 0.1 dynamic_slice.16
  191.2 0.1 reshape.33
  191.3 0.5 dynamic-slice_bitcast_fusion.live_ref
  191.8 26.5 %shard_map.78 = f32[8,2,1024,1024]{3,2,1,0:T(8,128)} custom-call(s32[8]{0:T(128)} %dynamic-slice_bitcast_fusion.live_ref, bf16[4,8,8,2,16,256]{5,4,3,2,1,0:T(8,128)(2,1)} %get-tuple-element.4.data_ref), custom_call_target="tpu_custom_call" | custom-call | flops 8589934592 | bytes 67108864 | tf_op jit(solution)/shard_map/pallas_call | solution.py:80
  218.3 25.0 %all-gather.2.cloned.1.call-done = bf16[256,128,128]{2,1,0:T(8,128)(2,1)} async-done(((bf16[32,128,128]{2,1,0:T(8,128)(2,1)}), bf16[256,128,128]{2,1,0:T(8,128)(2,1)}) %all-gather.2.cloned.1.call-update) | async-done | bytes 8388624 | tf_op jit(solution)/shard_map/all_gather | solution.py:519
  243.4 4.3 %gather_fusion.2 = bf16[64,128,128]{2,1,0:T(8,128)(2,1)S(1)} fusion(bf16[256,128,128]{2,1,0:T(8,128)(2,1)} %all-gather.2.cloned.1.call-done, s32[1024]{0:T(1024)S(1)} %pad_clamp_fusion), kind=kCustom, calls=%fused_computation.2 | custom fusion | bytes 4194560 | tf_op jit(solution)/shard_map/jit(_take)/gather | solution.py:527
  247.7 2.4 bitcast_convert_fusion
  (9 shorter events, 0.1 us)
Async XLA Ops:
  7.2 2.5 copy-start
  7.2 236.2 %all-gather.2.cloned.1.call-start = ((), (), s32[]{:S(2)}) async-start(), calls=%async_computation | async-start | bytes 9437184 | tf_op jit(solution)/shard_map/all_gather | solution.py:519
  26.4 164.1 %copy-start.1 = (s32[256]{0:T(256)S(1)}, s32[256]{0:T(256)}, u32[]{:S(2)}) copy-start(s32[256]{0:T(256)} %param.8) | copy-start | bytes 3076
Sparse Core Ops, SparseCore 0:
  190.5 52.8 all-gather.1

commit v4 on v3

--- a/solution.py
+++ b/solution.py
@@ -37,8 +37,17 @@
     return channel_of, live_slot
 
 
-def gram_kernel(scale, live_ref, data_ref, out_ref):
-    live = live_ref[pl.program_id(0)] > 0
+def gram_kernel(
+    scale, per_step, live_ref, here_ref, beam_live_ref, data_ref, *refs
+):
+    beam_refs = refs[:per_step]
+    out_ref, volt_ref = refs[per_step:]
+    slot = pl.program_id(0)
+    for j, beam_ref in enumerate(beam_refs):
+        alive = beam_live_ref[slot * per_step + j] > 0
+        volt_ref[j] = jnp.where(alive, beam_ref[0].astype(jnp.float32), 0.0)
+
+    live = live_ref[slot] > 0
 
     @pl.when(jnp.logical_not(live))
     def _():
@@ -74,27 +83,43 @@
             )
 
 
-def correlate(live, arrived, frames_total):
+def correlate(live, arrived, frames_total, here, beam_live, every):
     inps, chans, slots, _, frames, width = arrived.shape
     total = inps * width
+    beam_slots = here.shape[0]
+    per_step = beam_slots // slots
+    rows, lanes = every.shape[1:]
+
+    def beam_spec(j):
+        return pl.BlockSpec(
+            (1, rows, lanes), lambda s, live, here, beam_live: (here[s * per_step + j], 0, 0)
+        )
+
     return pl.pallas_call(
-        functools.partial(gram_kernel, 1.0 / frames_total),
+        functools.partial(gram_kernel, 1.0 / frames_total, per_step),
         grid_spec=pltpu.PrefetchScalarGridSpec(
-            num_scalar_prefetch=1,
+            num_scalar_prefetch=3,
             grid=(slots,),
             in_specs=[
-                pl.BlockSpec((inps, chans, 1, 2, frames, width), lambda s, live: (0, 0, s, 0, 0, 0))
+                pl.BlockSpec((inps, chans, 1, 2, frames, width), lambda s, *_: (0, 0, s, 0, 0, 0)),
+                *[beam_spec(j) for j in range(per_step)],
             ],
-            out_specs=pl.BlockSpec((1, 2, total, total), lambda s, live: (s, 0, 0, 0)),
+            out_specs=[
+                pl.BlockSpec((1, 2, total, total), lambda s, *_: (s, 0, 0, 0)),
+                pl.BlockSpec((per_step, rows, lanes), lambda s, *_: (s, 0, 0)),
+            ],
         ),
-        out_shape=jax.ShapeDtypeStruct((slots, 2, total, total), jnp.float32),
+        out_shape=[
+            jax.ShapeDtypeStruct((slots, 2, total, total), jnp.float32),
+            jax.ShapeDtypeStruct((beam_slots, rows, lanes), jnp.float32),
+        ],
         compiler_params=pltpu.CompilerParams(vmem_limit_bytes=VMEM_BYTES),
         cost_estimate=pl.CostEstimate(
             flops=slots * 2 * 2 * total * total * 2 * chans * frames,
             bytes_accessed=slots * 2 * total * total * 4,
             transcendentals=0,
         ),
-    )(live, arrived)
+    )(live, here, beam_live, arrived, *[every] * per_step)
 
 
 SIN_TERMS = [
@@ -126,6 +151,7 @@
     outgoing,
     delay_ref,
     arrived,
+    every,
     formed,
     data,
     middle,
@@ -146,6 +172,11 @@
     down_send,
     down_recv,
     own_sem,
+    spread_send,
+    spread_recv,
+    hand_send,
+    hand_recv,
+    keep_sem,
 ):
     inps = lax.axis_size("inp")
     chans = lax.axis_size("chan")
@@ -237,6 +268,51 @@
             device_id=(lax.rem(z + inps - 1, inps), me),
             device_id_type=MESH,
         )
+
+    sibling = me + 1 - 2 * lax.rem(me, 2)
+    chips = chans // 2
+
+    def spread_copy(p, g):
+        peer = sibling if p is None else lax.rem(me + 2 * p, chans)
+        slot = 0 if p is None else p
+        return pltpu.make_async_remote_copy(
+            src_ref=formed.at[rows_of(g)],
+            dst_ref=every.at[me, rows_of(g)],
+            send_sem=spread_send.at[slot, g],
+            recv_sem=spread_recv.at[slot, g],
+            device_id=(z, peer),
+            device_id_type=MESH,
+        )
+
+    def hand_copy(p, g):
+        source = lax.rem(me + chans - 2 * p, chans)
+        return pltpu.make_async_remote_copy(
+            src_ref=every.at[source, rows_of(g)],
+            dst_ref=every.at[source, rows_of(g)],
+            send_sem=hand_send.at[p, g],
+            recv_sem=hand_recv.at[p, g],
+            device_id=(z, sibling),
+            device_id_type=MESH,
+        )
+
+    def keep_copy(g):
+        return pltpu.make_async_copy(
+            formed.at[rows_of(g)], every.at[me, rows_of(g)], keep_sem.at[g]
+        )
+
+    def spread(g):
+        @pl.loop(1, chips)
+        def _(p):
+            spread_copy(p, g).start()
+
+        spread_copy(None, g).start()
+        keep_copy(g).start()
+
+    def hand_on(g):
+        @pl.loop(1, chips)
+        def _(p):
+            spread_copy(p, g).wait_recv()
+            hand_copy(p, g).start()
 
     own_data = pltpu.make_async_copy(mine.at[me], data.at[me], own_sem.at[inps])
     own_data.start()
@@ -368,7 +444,7 @@
                     total = total + down[d, rows].astype(jnp.float32)
                 formed[rows] = total.astype(jnp.bfloat16)
 
-    @pl.loop(0, groups + inps)
+    @pl.loop(0, groups + inps + 2)
     def _(turn):
         @pl.when(turn + 2 < groups)
         def _():
@@ -398,9 +474,14 @@
         def _():
             deal_on(turn - 2)
 
-        @pl.when(turn >= inps)
+        @pl.when((turn >= inps) & (turn - inps < groups))
         def _():
             finish(turn - inps)
+            spread(turn - inps)
+
+        @pl.when(turn >= inps + 2)
+        def _():
+            hand_on(turn - inps - 2)
 
     @pl.loop(0, chans)
     def _(q):
@@ -416,6 +497,14 @@
 
     @pl.loop(0, groups)
     def _(g):
+        keep_copy(g).wait()
+        spread_copy(None, g).wait()
+
+        @pl.loop(1, chips)
+        def _(p):
+            spread_copy(p, g).wait_send()
+            hand_copy(p, g).wait()
+
         @pl.loop(1, chans)
         def _(q):
             data_copy(g, q).wait_send()
@@ -449,13 +538,14 @@
         ],
         out_specs=[
             pl.BlockSpec(memory_space=pl.ANY),
-            pl.BlockSpec(memory_space=pltpu.VMEM),
+            pl.BlockSpec(memory_space=pl.ANY),
         ],
         out_shape=[
             jax.ShapeDtypeStruct(outgoing.shape, jnp.bfloat16),
-            jax.ShapeDtypeStruct(formed_shape, jnp.bfloat16),
+            jax.ShapeDtypeStruct((chans, *formed_shape), jnp.bfloat16),
         ],
         scratch_shapes=[
+            pltpu.VMEM(formed_shape, jnp.bfloat16),
             pltpu.VMEM(mine.shape, jnp.bfloat16),
             pltpu.VMEM(outgoing.shape, jnp.bfloat16),
             pltpu.VMEM((inps, *formed_shape), jnp.float32),
@@ -475,6 +565,11 @@
             dma((inps, groups)),
             dma((inps, groups)),
             dma((inps + 1,)),
+            dma((chans // 2, groups)),
+            dma((chans // 2, groups)),
+            dma((chans // 2, groups)),
+            dma((chans // 2, groups)),
+            dma((groups,)),
         ],
         compiler_params=pltpu.CompilerParams(
             collective_id=0, has_side_effects=True, vmem_limit_bytes=VMEM_BYTES
@@ -515,17 +610,13 @@
 
     delay_cols = lax.dynamic_slice_in_dim(delays, inp_here * input_count, input_count, 1)
     ordered = jnp.take(delay_cols, sections, axis=0, mode="clip").T
-    arrived, formed = exchange(mine, outgoing, ordered, length_total, all_inputs)
-    every = lax.all_gather(formed, "chan", axis=0, tiled=True)
-
-    visibilities = correlate(gram_live, arrived, all_frames)
-
     beam_channel, beam_live = slot_table(beam_owner, chan_count, beam_slots)
     here = lax.dynamic_slice_in_dim(beam_channel, chan_here * beam_slots, beam_slots)
-    live = lax.dynamic_slice_in_dim(beam_live, chan_here * beam_slots, beam_slots)
-    voltages = jnp.where(
-        live[:, None, None], jnp.take(every, here, axis=0, mode="clip"), jnp.zeros((), jnp.bfloat16)
-    ).astype(jnp.float32)
+    live = lax.dynamic_slice_in_dim(beam_live.astype(jnp.int32), chan_here * beam_slots, beam_slots)
+
+    arrived, every = exchange(mine, outgoing, ordered, length_total, all_inputs)
+    every = every.reshape(half_count, *every.shape[2:])
+    visibilities, voltages = correlate(gram_live, arrived, all_frames, here, live, every)
     return (visibilities, voltages[:, None])
 
 

time: 258 us -> 239 us (0.926)
  waiting for transfers between devices: 25.1 us -> 0 us
  Pallas kernels: 190 us -> 214 us
  between operations: 14.1 us -> 0.69 us
  local copies, waits for them, and re-layouts: 16.4 us -> 13.3 us
    all_gather x1 -> x0, waiting for transfers between devices: 25 us -> none  [shards(): every = lax.all_gather(formed, 'chan', axis=0, tiled=True)]
    pallas_call x1, Pallas kernels: 164 us -> 188 us  [exchange(): pl.pallas_call(functools.partial(exchange_kernel, length_total, 1.0 / mat...]
    gather x1 -> x0, local copies, waits for them, and re-layouts: 4.33 us -> none  [shards(): jnp.take(every, here, axis=0, mode='clip')]
  transfers between devices with their start and end apart: 1 -> 0, of which waited for: 1 -> 0; matrix products, arithmetic and copies ran while one was open for 1% -> 0% of each run, Pallas kernels for 10% -> 0%
where the time goes in v4:
time: 239 us; the launch traced here: 238 us
  Pallas kernels  214 us (90%)
  local copies, waits for them, and re-layouts  13.3 us (6%)
  matrix products  5.44 us (2%)
  other arithmetic  4.45 us (2%)
    pallas_call x1, Pallas kernels, exchange(): pl.pallas_call(functools.partial(exchange_kernel, length_total, 1.0 / mat...  188 us
    pallas_call x1, Pallas kernels, correlate(): pl.pallas_call(functools.partial(gram_kernel, 1.0 / frames_total, per_ste...  26.4 us
    dot_general x1, matrix products, shards(): jnp.einsum('kpw,ifw->kpfi', table, samples, preferred_element_type=jnp.fl...  5.44 us
    gather x1, local copies, waits for them, and re-layouts, shards(): jnp.take(spectra, gram_channel, axis=0, mode='clip')  5.02 us

profile of v4, /device:TPU:9, one launch (start us, length us, event | category | flops | bytes accessed | tf_op | source)
XLA Modules:
  0.0 238.2 jit_solution(15306711839648793237)
XLA Ops:
  0.6 0.0 copy-start
  0.7 0.9 convert_reduce_fusion.1
  1.6 0.7 multiply_add_fusion.1
  2.3 0.1 fusion.7
  2.4 0.1 select_reduce_fusion.1
  2.5 0.9 convert_reduce_fusion
  3.4 0.7 multiply_add_fusion
  4.1 0.2 fusion.5
  4.3 0.2 select_reduce_fusion
  4.4 0.7 dynamic_slice.14.here_ref
  5.1 0.7 dynamic_slice.15.beam_live_ref
  5.8 0.7 pad_clamp_fusion
  6.4 0.1 reshape.26
  6.5 0.6 dynamic-slice_bitcast_fusion.live_ref
  7.1 0.0 copy-done
  7.2 1.0 gather_fusion.1
  8.1 0.8 copy.21
  9.0 5.4 %convert_bitcast_fusion = bf16[256,2,16,256]{3,0,2,1:T(8,128)(2,1)S(1)} fusion(bf16[256,2,512,1]{2,0,3,1:T(8,128)(2,1)} %constant.32, bf16[256,16,512]{2,1,0:T(8,128)(2,1)} %param.6), kind=kOutput, calls=%fused_computation.5 | convolution fusion | flops 2149580800 | bytes 8912896 | tf_op jit(solution)/shard_map/kpw,ifw->kpfi/dot_general | solution.py:599
  14.4 4.4 %copy.19 = bf16[256,2,16,256]{3,2,1,0:T(8,128)(2,1)} copy(bf16[256,2,16,256]{3,0,2,1:T(8,128)(2,1)S(1)} %convert_bitcast_fusion) | data formatting | bytes 8388608 | tf_op jit(solution)/shard_map/convert_element_type | solution.py:601
  18.9 5.0 %gather_fusion = bf16[256,2,16,256]{3,2,1,0:T(8,128)(2,1)} fusion(bf16[256,2,16,256]{3,2,1,0:T(8,128)(2,1)} %copy.19, s32[1024]{0:T(1024)S(1)} %pad_clamp_fusion.1), kind=kCustom, calls=%fused_computation | custom fusion | bytes 8389632 | tf_op jit(solution)/shard_map/jit(_take)/gather | solution.py:605
  23.9 187.9 %shard_map.77 = (bf16[4,8,8,2,16,256]{5,4,3,2,1,0:T(8,128)(2,1)}, bf16[8,32,128,128]{3,2,1,0:T(8,128)(2,1)}) custom-call(bf16[8,32,2,16,256]{4,3,2,1,0:T(8,128)(2,1)} %bitcast.28, bf16[4,8,8,2,16,256]{5,4,3,2,1,0:T(8,128)(2,1)} %bitcast.29, f32[256,256]{1,0:T(8,128)} %bitcast.30), custom_call_target="tpu_custom_call" | custom-call | flops 2147483648 | bytes 8388608 | tf_op jit(solution)/shard_map/pallas_call | solution.py:532
  211.8 26.4 %shard_map.78 = (f32[8,2,1024,1024]{3,2,1,0:T(8,128)}, f32[64,128,128]{2,1,0:T(8,128)}) custom-call(s32[8]{0:T(128)} %dynamic-slice_bitcast_fusion.live_ref, s32[64]{0:T(128)} %dynamic_slice.14.here_ref, s32[64]{0:T(128)} %dynamic_slice.15.beam_live_ref, bf16[4,8,8,2,16,256]{5,4,3,2,1,0:T(8,128)(2,1)} %get-tuple-element.6.data_ref, ...), custom_call_target="tpu_custom_call" | custom-call | flops 8589934592 | bytes 67108864 | tf_op jit(solution)/shard_map/pallas_call | solution.py:98
  (4 shorter events, 0.0 us)
Async XLA Ops:
  0.6 6.5 %copy-start = (f32[256,1024]{1,0:T(8,128)S(1)}, f32[256,1024]{1,0:T(8,128)}, u32[]{:S(2)}) copy-start(f32[256,1024]{1,0:T(8,128)} %param.9) | copy-start | bytes 3145732
